TPU v7x, 32 devices: a whole 2x2x4 slice. The times are simulated.
32 devices in a mesh: mem: 4 (over z), patch: 8 (over y, x, core).
Axes of the slice: x: 2, y: 2, z: 4, core: 2. Of those that a mesh axis runs over, the one named last changes fastest.
Arguments:
- ensemble: bfloat16 [1024, 12, 4096], P(('mem', 'patch')), may hold values from -6 to 6
- obs_col: int32 [4096], replicated, may hold values from 0 to 4095, as said below
- obs_var: int32 [4096], replicated, may hold values from 0 to 11
- obs_value: float32 [4096], replicated, may hold values from -8 to 8
- obs_err: float32 [4096], replicated, may hold values from 0.5 to 2
- obs_count: int32 [32], replicated, may hold values from 32 to 128, as said below
- coarse_list: int32 [128, 128], P(('mem', 'patch')), may hold values from 0 to 383, as said below
- coarse_count: int32 [128], P(('mem', 'patch')), may hold values from 32 to 128, as said below
Outputs:
- analysis: bfloat16 [1024, 12, 4096], P(('mem', 'patch'))
Inputs may be any that keep to these rules, and one draw needn't show every extreme that they name: `obs_col`: slot j lies in column block j // 128, so its column is between (j // 128) * 128 and that plus 128 - 1. `obs_count`: patches whose index is 0 mod 4 hold 128 observations, those 2 mod 4 hold 32, the others between 64 and 128. `coarse_list`: entries of one row are distinct window rows of the coarse point's patch, all of present observations. `coarse_count`: the first coarse point of every patch uses all 128 slots.
All inputs are finite; a program needn't handle non-finite values. Where the computation divides by a largest or mean magnitude, that divisor is 1e-20 or more.
Results may differ from a plain program's by a relative error of at most 0.0017.
Values may be sent and summed in bfloat16 or wider, within the bound.
No kernel may reach another device: no remote copies, remote signals or barrier semaphores. Data moves between devices by JAX's collectives and lax.ppermute only.
A program may use at most 192 MiB of HBM per device.

v0:
```python
import jax
import jax.numpy as jnp
from jax import lax
from jax.sharding import PartitionSpec as P

OBS_DEV = 128
NS_STEPS = 4


def extended(array, sides, width):
    for axis, dim in sides:
        size, length = (lax.axis_size(axis), array.shape[dim])
        up = [(i, (i + 1) % size) for i in range(size)]
        down = [(j, i) for i, j in up]
        last = lax.slice_in_dim(array, length - width, length, axis=dim)
        leading = lax.slice_in_dim(array, 0, width, axis=dim)
        before = lax.ppermute(last, axis, up)
        after = lax.ppermute(leading, axis, down)
        array = jnp.concatenate([before, array, after], axis=dim)
    return array


def analyse(
    background,
    window_rows,
    values,
    errors,
    columns,
    present,
    lists,
    counts,
    first_column,
    total_columns,
):
    f32 = jnp.float32
    highest = lax.Precision.HIGHEST
    members, fields, col_count = background.shape
    blocks, slots = lists.shape
    group = col_count // blocks
    dof_ratio = members - 1.0
    wide = fields * col_count
    back_flat = background.reshape(members, wide)
    row_mean = jnp.mean(window_rows, axis=0, dtype=f32)
    obs_pert = (window_rows.astype(f32) - row_mean[None, :]).astype(jnp.bfloat16)
    innov = values - row_mean
    field_mean = jnp.mean(back_flat, axis=0, dtype=f32)
    pert_flat = (back_flat.astype(f32) - field_mean[None, :]).astype(jnp.bfloat16)
    live_slot = (jnp.arange(slots, dtype=jnp.int32)[None, :] < counts[:, None]) & present[lists]
    centre = (first_column + group * jnp.arange(blocks, dtype=jnp.int32)).astype(f32) + 0.5 * (
        group - 1
    )
    offset = columns[lists].astype(f32) - centre[:, None]
    offset = offset - total_columns * jnp.floor(offset / total_columns + 0.5)
    weight = jnp.where(live_slot, jnp.exp(-((offset / col_count) ** 2)) / errors[lists], 0.0)
    flat_list = lists.reshape(-1)
    picked = obs_pert[:, flat_list]
    full_gram = lax.dot_general(
        picked, picked, (((0,), (0,)), ((), ())), preferred_element_type=f32
    )
    block_ids = jnp.arange(blocks, dtype=jnp.int32)
    gram = full_gram.reshape(blocks, slots, blocks, slots)[block_ids, :, block_ids, :]
    identity = jnp.eye(slots, dtype=f32)
    bmat = identity + weight[:, :, None] * gram * weight[:, None, :] / dof_ratio
    scale = jnp.max(jnp.sum(jnp.abs(bmat), axis=2), axis=1)
    ymat = bmat / scale[:, None, None]
    zmat = jnp.broadcast_to(identity, bmat.shape)
    for newton_step in range(NS_STEPS):
        tmat = 0.5 * (3.0 * identity - jnp.matmul(zmat, ymat, precision=highest))
        ymat = jnp.matmul(ymat, tmat, precision=highest)
        zmat = jnp.matmul(tmat, zmat, precision=highest)
    root = jnp.sqrt(scale)[:, None, None] * ymat
    stacked = jnp.concatenate([bmat, bmat + root], axis=0)
    lowers = jnp.linalg.cholesky(stacked)
    inv_lowers = jax.scipy.linalg.solve_triangular(
        lowers, jnp.broadcast_to(identity, stacked.shape), lower=True
    )
    inv_b = inv_lowers[:blocks]
    inv_hl = inv_lowers[blocks:]
    inverse_h = jnp.matmul(jnp.swapaxes(inv_hl, 1, 2), inv_hl, precision=highest)
    rhs = weight * innov[lists]
    half = jnp.einsum("gij,gj->gi", inv_b, rhs, precision=highest)
    mean_weight = jnp.einsum("gji,gj->gi", inv_b, half, precision=highest) / dof_ratio
    mix = -(weight[:, :, None] * inverse_h * weight[:, None, :]) / dof_ratio
    shift_flat = (weight * mean_weight).reshape(-1)
    proj = lax.dot_general(picked, pert_flat, (((0,), (0,)), ((), ())), preferred_element_type=f32)
    own = (jnp.arange(blocks * slots, dtype=jnp.int32) // slots)[:, None] == (
        jnp.arange(col_count, dtype=jnp.int32) // group
    )[None, :]
    masked = jnp.where(
        own[:, None, :], proj.reshape(blocks * slots, fields, col_count), 0.0
    ).reshape(blocks * slots, wide)
    mean_term = jnp.dot(shift_flat, masked, precision=highest)
    eye_blocks = jnp.eye(blocks, dtype=f32)
    mix_full = (eye_blocks[:, None, :, None] * mix[:, :, None, :]).reshape(
        blocks * slots, blocks * slots
    )
    spread_term = lax.dot_general(
        mix_full, masked, (((0,), (0,)), ((), ())), precision=highest
    ).astype(jnp.bfloat16)
    update = jnp.dot(picked, spread_term, preferred_element_type=f32)
    total = back_flat.astype(f32) + mean_term[None, :] + update
    return total.astype(jnp.bfloat16).reshape(members, fields, col_count)


def shards(ensemble, obs_col, obs_var, obs_value, obs_err, obs_count, coarse_list, coarse_count):
    mem_count = lax.axis_size("mem")
    patch_count = lax.axis_size("patch")
    devices = mem_count * patch_count
    device_index = lax.axis_index(("mem", "patch"))
    local_members, fields, total_columns = ensemble.shape
    col_count = total_columns // devices
    background = lax.all_to_all(ensemble, ("mem", "patch"), split_axis=2, concat_axis=0, tiled=True)
    window_slot = jnp.arange(3 * OBS_DEV, dtype=jnp.int32)
    own_obs = device_index * OBS_DEV + jnp.arange(OBS_DEV, dtype=jnp.int32)
    flat_cells = obs_var[own_obs] * col_count + obs_col[own_obs] - device_index * col_count
    own_rows = background.reshape(local_members * devices, fields * col_count)[:, flat_cells]
    window_rows = extended(own_rows, ((("mem", "patch"), 1),), OBS_DEV)
    owner = (device_index - 1 + window_slot // OBS_DEV) % devices
    window_index = owner * OBS_DEV + window_slot % OBS_DEV
    present = window_slot % OBS_DEV < obs_count[owner]
    result = analyse(
        background,
        window_rows,
        obs_value[window_index],
        obs_err[window_index],
        obs_col[window_index],
        present,
        coarse_list,
        coarse_count,
        device_index * col_count,
        float(total_columns),
    )
    return lax.all_to_all(result, ("mem", "patch"), split_axis=0, concat_axis=2, tiled=True)


def solution(mesh):
    return jax.shard_map(
        shards,
        mesh=mesh,
        in_specs=(
            P(("mem", "patch"), None, None),
            P(),
            P(),
            P(),
            P(),
            P(),
            P(("mem", "patch"), None),
            P(("mem", "patch")),
        ),
        out_specs=P(("mem", "patch"), None, None),
        check_vma=False,
    )
```

profile of v0, /device:TPU:0, one launch (start us, length us, event | category | flops | bytes accessed | tf_op | source)
XLA Modules:
  0.0 524.2 jit_solution(6549575387268747298)
XLA Ops:
  0.0 18.2 %copy.100 = bf16[32,12,4096]{0,1,2:T(8,128)(2,1)} copy(bf16[32,12,4096]{2,0,1:T(8,128)(2,1)} %param.8) | data formatting | bytes 6291456 | tf_op args[0]
  18.2 18.9 %reshape.686 = bf16[32,2,24576]{2,1,0:T(2,128)(2,1)} reshape(bf16[4096,12,32]{2,1,0:T(8,128)(2,1)} %bitcast.149) | data formatting | bytes 6291456
  37.1 7.3 %all-to-all-start = ((bf16[32,2,24576]{2,1,0:T(2,128)(2,1)}), bf16[32,2,24576]{2,1,0:T(2,128)(2,1)S(1)}, u32[]{:S(2)}, u32[]{:S(2)}) async-start(bf16[32,2,24576]{2,1,0:T(2,128)(2,1)} %reshape.686), calls=%async_computation | async-start | bytes 6291456 | tf_op jit(solution)/shard_map/all_to_all | solution.py:112
  44.5 1.1 gather_fusion.6
  45.6 1.1 gather_fusion.5
  47.3 0.7 fusion.48
  48.0 4.4 fusion.39
  52.4 0.6 and_select_fusion.3
  52.9 0.5 convert_add_fusion.1
  53.5 0.6 add_select_fusion
  54.0 0.6 fusion.37
  54.7 0.6 pad_clamp_fusion
  55.3 0.6 iota_compare_fusion
  55.9 0.7 fusion.47
  56.6 0.6 fusion.26
  57.3 15.6 %fusion.27 = pred[384]{0:T(512)(128)(4,1)S(1)} fusion(pred[384]{0:T(512)(128)(4,1)S(1)} %get-tuple-element.45, pred[384]{0:T(512)(128)(4,1)S(1)} %get-tuple-element.46, pred[384]{0:T(512)(128)(4,1)S(1)} %get-tuple-element.47, pred[384]{0:T(512)(128)(4,1)S(1)} %get-tuple-element.48, pred[384]{0:T(512)(128)(4,1)S(1)} %get-tuple-element.49, ...), kind=kLoop, calls=%fused_computation.124 | loop fusion | flops 12288 | bytes 11620 | tf_op jit(solution)/shard_map/lt | solution.py:120
  72.9 43.0 %all-to-all-done = bf16[32,2,24576]{2,1,0:T(2,128)(2,1)S(1)} async-done(((bf16[32,2,24576]{2,1,0:T(2,128)(2,1)}), bf16[32,2,24576]{2,1,0:T(2,128)(2,1)S(1)}, u32[]{:S(2)}, u32[]{:S(2)}) %all-to-all-start) | async-done | bytes 3145760 | tf_op jit(solution)/shard_map/all_to_all | solution.py:112
  115.9 14.5 %reshape.687 = bf16[4096,12,32]{2,1,0:T(8,128)(2,1)} reshape(bf16[32,2,24576]{2,1,0:T(2,128)(2,1)S(1)} %all-to-all-done) | data formatting | bytes 6291456
  130.4 20.0 %copy.101 = bf16[32,12,32,128]{3,1,0,2:T(8,128)(2,1)} copy(bf16[32,12,32,128]{0,1,3,2:T(8,128)(2,1)} %bitcast.148) | data formatting | bytes 6291456 | tf_op jit(solution)/shard_map/all_to_all | solution.py:112
  150.4 3.4 convert_reduce_fusion
  153.9 3.4 fusion.3
  157.2 1.7 copy-done.6
  158.9 2.9 copy.103
  161.8 3.4 gather_fusion.7
  165.2 3.3 collective-permute-start.1
  168.5 0.4 collective-permute-start
  168.9 0.6 or_bitcast_fusion
  169.5 2.5 gather_fusion.1
  172.1 3.7 gather_fusion.10
  175.8 2.5 gather_fusion.3
  178.3 3.5 gather_fusion.4
  181.8 4.7 gather_fusion.2
  186.5 4.4 gather_fusion
  190.9 1.5 copy.102
  192.4 0.7 broadcast_compare_fusion
  193.1 2.8 copy.113
  196.0 1.2 convert_reduce_fusion.1
  197.2 3.5 gather_fusion.11
  200.7 1.2 fusion.4
  202.0 2.1 gather_fusion.8
  204.0 0.7 fusion.49
  205.4 0.6 gather_fusion.9
  206.5 0.8 fusion.9
  207.2 0.7 fusion.24
  207.9 0.7 fusion.21
  208.6 0.4 fusion.8
  209.8 0.4 fusion.7
  210.2 0.4 fusion.52
  211.0 0.4 fusion.6
  211.4 0.6 fusion.5
  212.4 93.8 %custom-call.8 = f32[8,128,128]{2,1,0:T(8,128)S(1)} custom-call(f32[8,128,128]{2,1,0:T(8,128)S(1)} %fusion.18), custom_call_target="Cholesky" | custom-call | tf_op jit(solution)/shard_map/jit(cholesky)/cholesky | solution.py:73
  306.5 78.8 %custom-call.9 = f32[8,1,128,128]{2,3,1,0:T(8,128)S(1)} custom-call(f32[8,1,128,128]{3,2,1,0:T(8,128)S(1)} %select_bitcast_fusion), custom_call_target="InvertDiagBlocksLowerTriangular" | custom-call | tf_op jit(solution)/shard_map/jit(_solve_triangular)/vmap()/triangular_solve | solution.py:74
  385.3 1.0 fusion.16
  386.2 0.6 fusion.12
  387.0 0.5 convolution_bitcast_fusion
  387.9 3.8 convolution_select_fusion
  391.9 10.2 %convolution_convert_fusion = bf16[512,1536]{1,0:T(8,128)(2,1)S(1)} fusion(f32[512,1536]{0,1:T(8,128)S(1)} %bitcast.153, f32[64,8,4,128]{3,2,1,0:T(4,128)S(1)} %bitcast.155), kind=kOutput, calls=%fused_computation.20 | convolution fusion | flops 4832624640 | bytes 5767168 | tf_op jit(solution)/shard_map/dot_general | solution.py:97
  402.1 2.7 convolution_reduce_fusion
  404.8 3.5 fusion.2
  408.4 3.2 copy.117
  411.6 7.7 %copy.118 = bf16[1024,12,128]{2,1,0:T(8,128)(2,1)} copy(bf16[1024,12,128]{0,2,1:T(8,128)(2,1)S(1)} %bitcast.152) | data formatting | bytes 6291456 | tf_op jit(solution)/shard_map/reshape | solution.py:102
  419.3 99.4 %all_to_all.33 = bf16[1024,12,128]{2,1,0:T(8,128)(2,1)S(1)} all-to-all(bf16[1024,12,128]{2,1,0:T(8,128)(2,1)} %copy.118), channel_id=1, replica_groups=mesh['mem'=4,'patch'=8] {'mem','patch'}, dimensions={0} | all-to-all | bytes 6291456 | tf_op jit(solution)/shard_map/all_to_all | solution.py:133
  518.6 2.0 copy.120
  520.6 3.3 all_to_all.30
  (96 shorter events, 4.1 us)
Async XLA Ops:
  0.0 44.5 %copy-start = (s32[4096]{0:T(1024)S(1)}, s32[4096]{0:T(1024)}, u32[]{:S(2)}) copy-start(s32[4096]{0:T(1024)} %param.9) | copy-start | bytes 49156
  37.1 8.5 %copy-start.5 = (s32[4096]{0:T(1024)S(1)}, s32[4096]{0:T(1024)}, u32[]{:S(2)}) copy-start(s32[4096]{0:T(1024)} %param.10) | copy-start | bytes 49156
  37.1 10.1 %copy-start.11 = (s32[32]{0:T(128)S(1)}, s32[32]{0:T(128)}, u32[]{:S(2)}) copy-start(s32[32]{0:T(128)} %param.13) | copy-start | bytes 388
  37.1 17.5 %copy-start.18 = (s32[4,128]{1,0:T(4,128)S(1)}, s32[4,128]{1,0:T(4,128)}, u32[]{:S(2)}) copy-start(s32[4,128]{1,0:T(4,128)} %param.14) | copy-start | bytes 6148
  37.1 78.8 %all-to-all-start = ((bf16[32,2,24576]{2,1,0:T(2,128)(2,1)}), bf16[32,2,24576]{2,1,0:T(2,128)(2,1)S(1)}, u32[]{:S(2)}, u32[]{:S(2)}) async-start(bf16[32,2,24576]{2,1,0:T(2,128)(2,1)} %reshape.686), calls=%async_computation | async-start | bytes 6291456 | tf_op jit(solution)/shard_map/all_to_all | solution.py:112
  150.4 3.4 copy-start.4
  157.2 1.7 copy-start.6
  161.8 10.2 %copy-start.2 = (f32[4096]{0:T(1024)S(1)}, f32[4096]{0:T(1024)}, u32[]{:S(2)}) copy-start(f32[4096]{0:T(1024)} %param.11) | copy-start | bytes 49156
  161.8 13.9 %copy-start.3 = (f32[4096]{0:T(1024)S(1)}, f32[4096]{0:T(1024)}, u32[]{:S(2)}) copy-start(f32[4096]{0:T(1024)} %param.12) | copy-start | bytes 49156
  165.2 30.8 %collective-permute-start.1 = (bf16[1024,128]{0,1:T(8,128)(2,1)S(1)}, bf16[1024,128]{0,1:T(8,128)(2,1)}, u32[]{:S(2)}, u32[]{:S(2)}) collective-permute-start(bf16[1024,128]{0,1:T(8,128)(2,1)S(1)} %bitcast.157), channel_id=1, source_target_pairs={{1,0},{2,1},{3,2},{4,3},{5,4},{6,5},{7,6},{8,7},{9,8},{10,9},{11,1... | collective-permute-start | bytes 786440 | tf_op jit(solution)/shard_map/ppermute | solution.py:18
  168.5 27.5 %collective-permute-start = (bf16[1024,128]{0,1:T(8,128)(2,1)S(1)}, bf16[1024,128]{0,1:T(8,128)(2,1)}, u32[]{:S(2)}, u32[]{:S(2)}) collective-permute-start(bf16[1024,128]{0,1:T(8,128)(2,1)S(1)} %bitcast.158), channel_id=1, source_target_pairs={{0,1},{1,2},{2,3},{3,4},{4,5},{5,6},{6,7},{7,8},{8,9},{9,10},{10,1... | collective-permute-start | bytes 786440 | tf_op jit(solution)/shard_map/ppermute | solution.py:17
  175.7 16.7 %copy-start.17 = (s32[512]{0:T(512)S(1)}, s32[512]{0:T(512)}, u32[]{:S(2)}) copy-start(s32[512]{0:T(512)} %add_select_fusion) | copy-start | bytes 6148
  175.7 16.7 %copy-start.22 = (s32[128]{0:T(128)S(1)}, s32[128]{0:T(128)}, u32[]{:S(2)}) copy-start(s32[128]{0:T(128)} %and_select_fusion.3) | copy-start | bytes 1540
  175.7 17.4 %copy-start.8 = (bf16[1536,1024]{0,1:T(8,128)(2,1)S(1)}, bf16[1536,1024]{0,1:T(8,128)(2,1)}, u32[]{:S(2)}) copy-start(bf16[1536,1024]{0,1:T(8,128)(2,1)} %get-tuple-element.9) | copy-start | bytes 9437188
  193.1 4.1 copy-start.20
  196.0 6.0 %copy-start.14 = (s32[1024]{0:T(1024)S(1)}, s32[1024]{0:T(1024)}, u32[]{:S(2)}) copy-start(s32[1024]{0:T(1024)} %pad_clamp_fusion) | copy-start | bytes 12292
  204.0 1.3 copy-start.15
  204.8 1.3 copy-start.19
  204.8 1.3 copy-start.21
  204.8 1.3 copy-start.23
  204.8 1.3 copy-start.24
  204.8 1.3 copy-start.9
  210.6 95.6 %copy-start.12 = (pred[128,128]{1,0:T(8,128)(4,1)S(1)}, pred[128,128]{1,0:T(8,128)(4,1)}, u32[]{:S(2)}) copy-start(pred[128,128]{1,0:T(8,128)(4,1)} %iota_compare_fusion) | copy-start | bytes 49156
  211.4 173.8 %copy-start.10 = (f32[128,128]{1,0:T(8,128)S(1)}, f32[128,128]{1,0:T(8,128)}, u32[]{:S(2)}) copy-start(f32[128,128]{1,0:T(8,128)} %fusion.26) | copy-start | bytes 196612
  212.3 175.6 %copy-start.13 = (pred[512,128]{0,1:T(8,128)(4,1)S(1)}, pred[512,128]{0,1:T(8,128)(4,1)}, u32[]{:S(2)}) copy-start(pred[512,128]{0,1:T(8,128)(4,1)} %broadcast_compare_fusion) | copy-start | bytes 196612
  387.9 3.8 copy-start.16
  402.1 2.7 copy-start.7
  518.6 5.3 %copy-start.1 = (s32[4096]{0:T(1024)S(1)}, s32[4096]{0:T(1024)}, u32[]{:S(2)}) copy-start(s32[4096]{0:T(1024)} %param.9) | copy-start | bytes 49156
where the time goes:
time: 533 us; the launch traced here: 524 us
  other arithmetic  209 us (39%)
  local copies, waits for them, and re-layouts  132 us (25%)
  blocking collectives  99.4 us (19%)
  waiting for transfers between devices  43 us (8%)
  matrix products  28.9 us (5%)
  starting transfers between devices  11 us (2%)
    all_to_all x1, blocking collectives, shards(): lax.all_to_all(result, ('mem', 'patch'), split_axis=0, concat_axis=2, til...  99.4 us
    another operation x4, other arithmetic, analyse(): lowers = jnp.linalg.cholesky(stacked)  94.6 us
    another operation x3, other arithmetic, analyse(): jax.scipy.linalg.solve_triangular(lowers, jnp.broadcast_to(identity, stac...  78.9 us
    unnamed x53, local copies, waits for them, and re-layouts  53.4 us
    all_to_all x1, waiting for transfers between devices, shards(): lax.all_to_all(ensemble, ('mem', 'patch'), split_axis=2, concat_axis=0, t...  43 us
    all_to_all x1, local copies, waits for them, and re-layouts, shards(): lax.all_to_all(ensemble, ('mem', 'patch'), split_axis=2, concat_axis=0, t...  20 us
    lt x1, other arithmetic, shards(): present = window_slot % OBS_DEV < obs_count[owner]  15.6 us
  transfers between devices with their start and end apart: 3, of which 1 were waited for; matrix products, arithmetic and copies ran while one was open for 11% of the time, Pallas kernels for 0%

commit v1 on v0

v1 whole, which is shorter than its diff:
```python
import functools

import jax
import jax.numpy as jnp
from jax import lax
from jax.experimental import pallas as pl
from jax.experimental.pallas import tpu as pltpu
from jax.sharding import PartitionSpec as P

OBS_DEV = 128
TAIL = 16
NS_STEPS = 4
AXES = ("mem", "patch")
MIB = 1 << 20
F32 = jnp.float32
BF16 = jnp.bfloat16


def dot16(left, right):
    return lax.dot_general(left, right, (((1,), (0,)), ((), ())), preferred_element_type=F32)


def thirds(value):
    high = value.astype(BF16)
    rest = value - high.astype(F32)
    middle = rest.astype(BF16)
    return high, middle, (rest - middle.astype(F32)).astype(BF16)


def stacked(right):
    high, middle, low = thirds(right)
    return jnp.concatenate([high, middle], axis=0), jnp.concatenate([low, high], axis=0)


def dot32(left, right):
    first, second = right if isinstance(right, tuple) else stacked(right)
    high, middle, low = thirds(left)
    large = dot16(jnp.concatenate([high, high], axis=1), first)
    small = dot16(jnp.concatenate([middle, middle], axis=1), first)
    return large + (small + dot16(jnp.concatenate([high, low], axis=1), second))


def invert_all(a_ref, width):
    matrices, size, _ = a_ref.shape
    count = size // width
    packs = [range(first, first + count) for first in range(0, matrices, count)]
    row = lax.broadcasted_iota(jnp.int32, (size, size), 0)
    lane = lax.broadcasted_iota(jnp.int32, (size, size), 1)
    sub_small = lax.broadcasted_iota(jnp.int32, (width, size), 0)
    lane_small = lax.broadcasted_iota(jnp.int32, (width, size), 1)
    segment = lane_small // width
    within = lane_small - segment * width
    diagonal = (row // width) == (lane // width)
    minus_unit = -((row == lane).astype(F32))

    def block(j, carry):
        start = pl.multiple_of(j * width, width)
        turns = [lax.rem(m * width + size - start, size) for m in range(count)]
        slabs, tops = [], []
        for pack in packs:
            slab = [a_ref[m, pl.ds(start, width), :] for m in pack]
            packed = jnp.zeros((width, size), F32)
            for m in range(count):
                packed = jnp.where(segment == m, pltpu.roll(slab[m], turns[m], 1), packed)
            slabs.append(slab)
            tops.append(packed)
        for k in range(0, width, 2):
            for p, packed in enumerate(tops):
                one = jnp.take_along_axis(packed, segment * width + k, axis=1)
                two = jnp.take_along_axis(packed, segment * width + (k + 1), axis=1)
                a, b = one[k : k + 1, :], two[k : k + 1, :]
                c, d = one[k + 1 : k + 2, :], two[k + 1 : k + 2, :]
                scale = 1.0 / (a * d - b * c)
                at = within[0:1, :]
                upper = jnp.where((at == k) | (at == k + 1), 0.0, packed[k : k + 1, :])
                upper = jnp.where(at == k, 1.0, upper)
                lower = jnp.where((at == k) | (at == k + 1), 0.0, packed[k + 1 : k + 2, :])
                lower = jnp.where(at == k + 1, 1.0, lower)
                first = (d * upper - b * lower) * scale
                second = (a * lower - c * upper) * scale
                pair = (sub_small == k) | (sub_small == k + 1)
                one = jnp.where(pair, jnp.where(sub_small == k, -1.0, 0.0), one)
                two = jnp.where(pair, jnp.where(sub_small == k, 0.0, -1.0), two)
                rest = jnp.where(pair | (within == k) | (within == k + 1), 0.0, packed)
                tops[p] = rest - (one * first + two * second)
        here = lane_small - start
        inside = (here >= 0) & (here < width)
        unit = (here == sub_small).astype(F32)
        in_row = (row >= start) & (row < start + width)
        in_lane = (lane >= start) & (lane < start + width)
        for pack, slab, packed in zip(packs, slabs, tops):
            left = jnp.where(diagonal, jnp.concatenate([packed] * count, axis=0), 0.0)
            right = jnp.concatenate([jnp.where(inside, unit, each) for each in slab], axis=0)
            strip = stacked(dot32(left, right))
            for i, m in enumerate(pack):
                full = a_ref[m]
                head = jnp.where(in_lane, jnp.where(in_row, minus_unit, full), 0.0)
                head = pltpu.roll(head, turns[i], 1)
                a_ref[m] = jnp.where(in_row | in_lane, 0.0, full) - dot32(head, strip)
        return carry

    lax.fori_loop(0, size // width, block, 0)


def parts_of(value):
    parts = []
    for _ in range(3):
        part = value.astype(BF16).astype(F32)
        parts.append(part)
        value = value - part
    return parts


def sum_units(fields, members):
    return -(-3 * fields // members)


def split_kernel(per_step, width, ens_ref, var_ref, col_ref, send_ref, later_ref, head_ref, sems):
    half, _, units, _, _ = send_ref.shape
    devices = 2 * half
    later = later_ref.shape[2]
    fields, members, _ = ens_ref.shape
    early = fields - later
    extra = units - 3 - early
    step = pl.program_id(0)
    copies = []
    for q in range(per_step):
        patch = step * per_step + q
        spot = (lax.rem(patch, half), patch // half)
        lanes = slice(q * width, (q + 1) * width)
        first = send_ref.at[spot[0], spot[1], pl.ds(3 + extra, early)]
        second = later_ref.at[spot[0], spot[1]]
        copies += [
            pltpu.make_async_copy(ens_ref.at[:early, :, lanes], first, sems.at[0, q]),
            pltpu.make_async_copy(ens_ref.at[early:, :, lanes], second, sems.at[1, q]),
        ]
    for copy in copies:
        copy.start()
    place = lax.broadcasted_iota(jnp.int32, (width, OBS_DEV), 0)
    for q in range(per_step):
        patch = step * per_step + q
        spot = (lax.rem(patch, half), patch // half)
        piece = ens_ref[:, :, q * width : (q + 1) * width]
        wide = piece.astype(F32)
        parts = parts_of(jnp.sum(wide[early:], axis=1))
        parts.append(jnp.zeros((extra * members - 3 * later, width), F32))
        parts = jnp.concatenate(parts, axis=0).astype(BF16)
        for u in range(extra):
            head_ref[spot[0], spot[1], 3 + u] = parts[u * members : (u + 1) * members]
        column = col_ref[pl.ds(patch, 1), :] - patch * width
        variable = var_ref[pl.ds(patch, 1), :]
        pick = (place == column).astype(F32).astype(BF16)
        values = dot16(wide.reshape(fields * members, width).astype(BF16), pick)
        taken = jnp.zeros((members, OBS_DEV), F32)
        for f in range(fields):
            taken = jnp.where(variable == f, values[f * members : (f + 1) * members], taken)
        taken = taken.astype(BF16)
        for b in range(3):
            window = lax.rem(patch + (devices + 1 - b), devices)
            head_ref[lax.rem(window, half), window // half, b] = taken
    for copy in copies:
        copy.wait()

    @pl.when(step == devices // per_step - 1)
    def _():
        target = send_ref.at[:, :, pl.ds(0, 3 + extra)]
        copy = pltpu.make_async_copy(head_ref, target, sems.at[0, 0])
        copy.start()
        copy.wait()


def split(ensemble, obs_var, obs_col, devices, early):
    fields, members, columns = ensemble.shape
    width = columns // devices
    per_step = 8
    later = fields - early
    units = (3 + sum_units(later, members) + early, later)
    shapes = [(devices // 2, 2, count, members, width) for count in units]
    return pl.pallas_call(
        functools.partial(split_kernel, per_step, width),
        grid=(devices // per_step,),
        in_specs=[
            pl.BlockSpec((fields, members, per_step * width), lambda i: (0, 0, i)),
            pl.BlockSpec((devices, OBS_DEV), lambda i: (0, 0)),
            pl.BlockSpec((devices, OBS_DEV), lambda i: (0, 0)),
        ],
        out_specs=[pl.BlockSpec(memory_space=pltpu.HBM)] * 2,
        out_shape=[jax.ShapeDtypeStruct(shape, BF16) for shape in shapes],
        scratch_shapes=[
            pltpu.VMEM((devices // 2, 2, units[0] - early, members, width), BF16),
            pltpu.SemaphoreType.DMA((2, per_step)),
        ],
        compiler_params=pltpu.CompilerParams(vmem_limit_bytes=56 * MIB),
        name="split",
    )(ensemble, obs_var, obs_col)


def call(kernel, name, outs, scalars, arrays, scratch=(), flops=10**9):
    whole = lambda array: pl.BlockSpec(array.shape, lambda i: (0,) * len(array.shape))
    outs = [jax.ShapeDtypeStruct(shape, dtype) for shape, dtype in outs]
    return pl.pallas_call(
        kernel,
        grid=(1,),
        in_specs=[pl.BlockSpec(memory_space=pltpu.SMEM)] * len(scalars)
        + [whole(array) for array in arrays],
        out_specs=[whole(out) for out in outs],
        out_shape=outs,
        scratch_shapes=list(scratch),
        compiler_params=pltpu.CompilerParams(vmem_limit_bytes=24 * MIB),
        cost_estimate=pl.CostEstimate(flops=flops, bytes_accessed=MIB, transcendentals=0),
        name=name,
    )(*scalars, *arrays)


def sums_kernel(later, side_ref, x_ref, lists_ref, out_ref, copy_ref):
    _, _, units, local, width = x_ref.shape
    extra = sum_units(later, local)
    copy_ref[...] = x_ref[...]
    for r in range(2):
        whole = jnp.sum(x_ref[:, side_ref[0] ^ r].astype(F32), axis=0)
        parts = whole[3 : 3 + extra].reshape(extra * local, width)
        out_ref[r, 0:3] = jnp.sum(whole[0:3], axis=1)
        early = units - extra
        out_ref[r, 3:early] = jnp.sum(whole[3 + extra :], axis=1)
        total = (parts[0:later] + parts[later : 2 * later]) + parts[2 * later : 3 * later]
        out_ref[r, early : early + later] = total
        out_ref[r, early + later :] = lists_ref[...].astype(F32)


def sums(side, x, lists, later):
    _, _, units, local, width = x.shape
    rows = units - sum_units(later, local) + later + lists.shape[0]
    outs = [((2, rows, width), F32), (x.shape, BF16)]
    return call(functools.partial(sums_kernel, later), "sums", outs, [side], [x, lists])


def picks_kernel(r, side_ref, rows_ref, sum_ref, got_ref, lists_ref, *out_refs):
    picked_ref, turned_ref, gram_ref, *mean_refs = out_refs
    half, _, _, local, _ = rows_ref.shape
    members = half * local
    blocks, slots = lists_ref.shape
    after = sum_ref.shape[1] - blocks
    window_row = lax.broadcasted_iota(jnp.int32, (3 * OBS_DEV, slots), 0)
    mean = (sum_ref[r, 0:3] + got_ref[1 - r, 0:3]) / (2 * members)
    lists = got_ref[0, after:].astype(jnp.int32) if r else lists_ref[...]
    for mean_ref in mean_refs:
        mean_ref[...] = mean
    perts, grams = [], []
    for b in range(3):
        rows = rows_ref[:, side_ref[0] ^ r, b].astype(F32).reshape(members, OBS_DEV)
        perts.append((rows - mean[b : b + 1, :]).astype(BF16))
    pert = jnp.concatenate(perts, axis=1)
    for g in range(blocks):
        choose = (window_row == lists[g : g + 1, :]).astype(F32).astype(BF16)
        picked32 = dot16(pert, choose)
        picked = picked32.astype(BF16)
        turned = picked32.T.astype(BF16)
        piece = slice(g * slots, (g + 1) * slots)
        picked_ref[:, piece] = picked
        turned_ref[piece, :] = turned
        grams.append(dot16(turned, picked))
    if r == 0:
        gram_ref[...] = jnp.concatenate(grams, axis=0)
        return
    lane = lax.broadcasted_iota(jnp.int32, (slots, slots), 1)
    row = lax.broadcasted_iota(jnp.int32, (slots, slots), 0)
    rest = []
    for g in range(0, blocks, 2):
        piece = slice(g // 2 * slots, (g // 2 + 1) * slots)
        gram_ref[piece, :] = jnp.where(row <= lane, grams[g], grams[g + 1])
        diagonal = jnp.where(row == lane, grams[g + 1], 0.0)
        rest.append(jnp.sum(diagonal, axis=0, keepdims=True))
    rest.append(jnp.zeros((8 - blocks // 2, slots), F32))
    gram_ref[blocks // 2 * slots :, :] = jnp.concatenate(rest, axis=0)


def picks(r, side, rows, total, got, lists):
    half, _, _, local, _ = rows.shape
    blocks, slots = lists.shape
    members, wide = half * local, blocks * slots
    outs = [((members, wide), BF16), ((wide, members), BF16)]
    outs += [((wide // 2 + 8, slots), F32)] if r else [((wide, slots), F32), ((3, OBS_DEV), F32)]
    kernel = functools.partial(picks_kernel, r)
    return call(kernel, "picks", outs, [side], [rows, total, got, lists], flops=2 * 10**9)


def weights_kernel(
    members,
    total_columns,
    me_ref,
    obs_count_ref,
    live_ref,
    lists_ref,
    value_ref,
    err_ref,
    col_ref,
    mean_ref,
    gram_ref,
    got_ref,
    mix_ref,
    shift_ref,
    a_ref,
):
    devices = value_ref.shape[0]
    blocks, slots = lists_ref.shape
    col_count = shift_ref.shape[1]
    group = col_count // blocks
    dof = members - 1.0
    window = 3 * OBS_DEV
    me = me_ref[0]
    lane_row = lax.broadcasted_iota(jnp.int32, (1, OBS_DEV), 1)
    means, values, errors, columns, presents = [], [], [], [], []
    for b in range(3):
        owner = lax.rem(me + (b - 1 + devices), devices)
        means.append(mean_ref[b : b + 1, :])
        values.append(value_ref[pl.ds(owner, 1), :])
        errors.append(err_ref[pl.ds(owner, 1), :])
        columns.append(col_ref[pl.ds(owner, 1), :].astype(F32))
        presents.append((lane_row < obs_count_ref[owner]).astype(F32))
    table = jnp.concatenate(
        [jnp.concatenate(x, axis=1) for x in (values, errors, columns, presents, means)]
        + [jnp.zeros((3, window), F32)],
        axis=0,
    )
    lane = lax.broadcasted_iota(jnp.int32, (slots, slots), 1)
    row = lax.broadcasted_iota(jnp.int32, (slots, slots), 0)
    unit = (row == lane).astype(F32)
    window_row = lax.broadcasted_iota(jnp.int32, (window, slots), 0)
    bmats, scales, wides, rhs = [], [], [], []
    for g in range(blocks):
        choose = (window_row == lists_ref[g : g + 1, :]).astype(F32)
        listed = dot32(table, choose)
        value, error, column, present, mean = [listed[i : i + 1, :] for i in range(5)]
        first = (me * col_count + group * g).astype(F32) + 0.5 * (group - 1)
        offset = column - first
        offset = offset - total_columns * jnp.floor(offset / total_columns + 0.5)
        live = (lane_row < live_ref[g]) & (present > 0.5)
        weight = jnp.where(live, jnp.exp(-((offset / col_count) ** 2)) / error, 0.0)
        rhs.append(weight * (value - mean))
        wide = jnp.broadcast_to(weight, (slots, slots))
        wides.append((wide, wide.T))
        piece = slice(g * slots, (g + 1) * slots)
        square = got_ref[g // 2 * slots : (g // 2 + 1) * slots, :]
        if g % 2 == 0:
            other = jnp.where(row <= lane, square, square.T)
        else:
            place = blocks // 2 * slots + g // 2
            other = jnp.where(row > lane, square, square.T)
            other = jnp.where(row == lane, got_ref[place : place + 1, :], other)
        gram = gram_ref[piece, :] + other
        bmat = unit + wides[g][1] * gram * wide / dof
        scales.append(jnp.max(jnp.sum(jnp.abs(bmat), axis=0, keepdims=True), axis=1, keepdims=True))
        bmats.append(bmat)
    every = range(blocks)
    ymats = [bmats[g] / scales[g] for g in every]
    zmats = [None] * blocks
    for step in range(NS_STEPS):
        if step == 0:
            tmats = [0.5 * (3.0 * unit - ymats[g]) for g in every]
        else:
            products = [dot32(zmats[g], ymats[g]) for g in every]
            tmats = [0.5 * (3.0 * unit - products[g]) for g in every]
        ymats = [dot32(ymats[g], tmats[g]) for g in every]
        if step == 0:
            zmats = tmats
        elif step < NS_STEPS - 1:
            zmats = [dot32(tmats[g], zmats[g]) for g in every]
    for g in every:
        a_ref[g] = bmats[g]
        a_ref[blocks + g] = bmats[g] + jnp.sqrt(scales[g]) * ymats[g]
    invert_all(a_ref, slots // blocks)
    shift = jnp.zeros((slots, col_count), F32)
    group_of = lax.broadcasted_iota(jnp.int32, (slots, col_count), 1) // group
    for g in every:
        wide, tall = wides[g]
        mean_weight = jnp.sum(a_ref[g] * rhs[g], axis=1, keepdims=True) / dof
        shift = jnp.where(group_of == g, tall[:, 0:1] * mean_weight, shift)
        mix = -(tall * a_ref[blocks + g] * wide) / dof
        mix_ref[g * slots : (g + 1) * slots, :] = mix.T
    shift_ref[...] = shift


def weights(me, obs_count, live, lists, value, err, col, mean, gram, got, members, total):
    blocks, slots = lists.shape
    width = total // value.shape[0]
    outs = [((blocks * slots, slots), F32), ((slots, width), F32)]
    return call(
        functools.partial(weights_kernel, members, float(total)),
        "weights",
        outs,
        [me, obs_count, live],
        [lists, value, err, col, mean, gram, got],
        [pltpu.VMEM((2 * blocks, slots, slots), F32)],
        flops=8 * 10**10,
    )


def lane_groups(slots, some, width, blocks):
    place = lax.broadcasted_iota(jnp.int32, (slots, some * width), 1)
    return lax.rem(place // (width // blocks), blocks)


def own_blocks(tall, group_of, blocks):
    slots = group_of.shape[0]
    own = tall[0:slots]
    for g in range(1, blocks):
        own = jnp.where(group_of == g, tall[g * slots : (g + 1) * slots], own)
    return own


def side_by_side(x_ref, j, first, some):
    half, _, _, local, width = x_ref.shape
    rows = half * local
    pieces = [x_ref[:, j, first + i].astype(F32).reshape(rows, width) for i in range(some)]
    return jnp.concatenate(pieces, axis=1)


def project_kernel(blocks, first, row, side_ref, x_ref, *rest):
    sum_ref, got_ref, turned_ref, turned_theirs_ref, mine_ref, theirs_ref = rest
    half, _, units, local, width = x_ref.shape
    members = half * local
    some = units - first
    group_of = lane_groups(mine_ref.shape[0], some, width, blocks)
    sides = ((1, turned_theirs_ref, theirs_ref), (0, turned_ref, mine_ref))
    for r, turn_ref, out_ref in sides:
        mean = (sum_ref[r] + got_ref[1 - r]) / (2 * members)
        mean = jnp.concatenate([mean[row + i : row + i + 1, :] for i in range(some)], axis=1)
        pert = (side_by_side(x_ref, side_ref[0] ^ r, first, some) - mean).astype(BF16)
        own = own_blocks(dot16(turn_ref[...], pert), group_of, blocks)
        out_ref[...] = own.astype(out_ref.dtype)


def project(side, x, sum_x, got_x, turned, turned_theirs, blocks, first, row):
    _, _, units, _, width = x.shape
    shape = (turned.shape[0] // blocks, (units - first) * width)
    kernel = functools.partial(project_kernel, blocks, first, row)
    arrays = [x, sum_x, got_x, turned, turned_theirs]
    return call(kernel, "project", [(shape, F32), (shape, BF16)], [side], arrays, flops=2 * 10**9)


def spread_kernel(blocks, mine_ref, got_ref, mix_ref, shift_ref, out_ref):
    slots, width = shift_ref.shape
    lanes = mine_ref.shape[1]
    some = lanes // width
    own = mine_ref[...] + got_ref[...].astype(F32)
    group_of = lane_groups(slots, some, width, blocks)
    shift = jnp.concatenate([shift_ref[...]] * some, axis=1)
    rest = jnp.sum(shift * own, axis=0, keepdims=True)
    out_ref[0:slots, :] = own_blocks(dot32(mix_ref[...], own), group_of, blocks).astype(BF16)
    parts = parts_of(rest) + [jnp.zeros((TAIL - 3, lanes), F32)]
    out_ref[slots:, :] = jnp.concatenate(parts, axis=0).astype(BF16)


def spread(mine, got, mix, shift, blocks):
    slots, lanes = mine.shape
    outs = [((slots + TAIL, lanes), BF16)]
    kernel = functools.partial(spread_kernel, blocks)
    return call(kernel, "spread", outs, [], [mine, got, mix, shift], flops=2 * 10**9)[0]


def update_kernel(blocks, first, side_ref, x_ref, *rest):
    picked_ref, picked_theirs_ref, mine_ref, theirs_ref, out_ref = rest
    half, _, some, local, width = out_ref.shape
    slots = mine_ref.shape[0] - TAIL
    group_of = lane_groups(slots, some, width, blocks)
    sides = ((picked_ref, mine_ref), (picked_theirs_ref, theirs_ref))
    for r, (pick_ref, term_ref) in enumerate(sides):
        j = side_ref[0] ^ r
        terms = term_ref[0:slots, :].astype(F32)
        parts = [jnp.where(group_of == g, terms, 0.0).astype(BF16) for g in range(blocks)]
        update = dot16(pick_ref[...], jnp.concatenate(parts, axis=0))
        tail = term_ref[slots:, :].astype(F32)
        mean_term = (tail[0:1, :] + tail[1:2, :]) + tail[2:3, :]
        result = (side_by_side(x_ref, j, first, some) + mean_term) + update
        for i in range(some):
            piece = result[:, i * width : (i + 1) * width]
            out_ref[:, j, i] = piece.reshape(half, local, width).astype(BF16)


def update(side, x, picked, picked_theirs, terms, got_terms, blocks, first):
    half, two, _, local, width = x.shape
    some = terms.shape[1] // width
    kernel = functools.partial(update_kernel, blocks, first)
    outs = [((half, two, some, local, width), BF16)]
    arrays = [x, picked, picked_theirs, terms, got_terms]
    return call(kernel, "update", outs, [side], arrays, flops=2 * 10**9)[0]


def join_kernel(in_ref, *rest):
    out_ref = rest[-1]
    per_step, _, _, _, width = in_ref.shape
    for q in range(per_step):
        out_ref[:, :, q * width : (q + 1) * width] = in_ref[q, 0]


def join(pieces, chunk, chunks, before):
    half, _, some, local, width = pieces.shape
    per_step = 16 if half % 16 == 0 else half
    steps = half // per_step
    operands = [pieces]
    in_specs = [
        pl.BlockSpec(
            (per_step, 1, some, local, width),
            lambda i: (lax.rem(i, steps), i // steps, 0, 0, 0),
        )
    ]
    if before is not None:
        operands.append(before)
        in_specs.append(pl.BlockSpec(memory_space=pl.ANY))
    return pl.pallas_call(
        join_kernel,
        grid=(2 * steps,),
        in_specs=in_specs,
        out_specs=pl.BlockSpec((some, local, per_step * width), lambda i: (chunk, 0, i)),
        out_shape=jax.ShapeDtypeStruct((some * chunks, local, 2 * half * width), BF16),
        input_output_aliases={} if before is None else {1: 0},
        compiler_params=pltpu.CompilerParams(vmem_limit_bytes=24 * MIB),
        name="join",
    )(*operands)


def shards(ensemble, obs_col, obs_var, obs_value, obs_err, obs_count, coarse_list, coarse_count):
    devices = lax.axis_size("mem") * lax.axis_size("patch")
    half = devices // 2
    me = lax.axis_index(AXES).astype(jnp.int32).reshape(1)
    side = me // half
    local, fields, total = ensemble.shape
    blocks = coarse_list.shape[0]
    by_patch = lambda array: array.reshape(devices, OBS_DEV)
    early = fields // 2
    later = fields - early
    swap = functools.partial(
        lax.all_to_all,
        axis_name=AXES,
        split_axis=0,
        concat_axis=0,
        tiled=True,
        axis_index_groups=[list(range(half)), list(range(half, devices))],
    )
    pairs = [(i, (i + half) % devices) for i in range(devices)]
    cross = lambda array: lax.ppermute(array, AXES, pairs)
    tie = lax.optimization_barrier

    ours = jnp.transpose(ensemble, (1, 0, 2))
    send0, send1 = split(ours, by_patch(obs_var), by_patch(obs_col), devices, early)
    skip = 3 + sum_units(later, local)
    sum_x, x0 = sums(side, swap(send0), coarse_list, later)
    got_x = cross(sum_x)
    picked_theirs, turned_theirs, gram_theirs = picks(1, side, x0, sum_x, got_x, coarse_list)
    got_gram = cross(gram_theirs)
    picked, turned, gram, mean = picks(0, side, x0, sum_x, got_x, coarse_list)
    turns = (sum_x, got_x, turned, turned_theirs, blocks)
    mine0, other0 = project(side, x0, *turns, skip, 3)
    got_other0 = cross(other0)
    got_gram, mine0, send1 = tie((got_gram, mine0, send1))
    x1 = swap(send1)
    mix, shift = weights(
        me,
        obs_count,
        coarse_count,
        coarse_list,
        by_patch(obs_value),
        by_patch(obs_err),
        by_patch(obs_col),
        mean,
        gram,
        got_gram,
        local * devices,
        total,
    )
    terms0 = spread(mine0, got_other0, mix, shift, blocks)
    got_terms0 = cross(terms0)
    terms0, x1 = tie((terms0, x1))
    mine1, other1 = project(side, x1, *turns, 0, 3 + early)
    got_other1 = cross(other1)
    result0 = update(side, x0, picked, picked_theirs, terms0, got_terms0, blocks, skip)
    result0, got_other1 = tie((result0, got_other1))
    terms1 = spread(mine1, got_other1, mix, shift, blocks)
    back0 = swap(result0)
    result1 = update(side, x1, picked, picked_theirs, terms1, cross(terms1), blocks, 0)
    result = join(swap(result1), 1, 2, join(back0, 0, 2, None))
    return jnp.transpose(result, (1, 0, 2))


def solution(mesh):
    return jax.shard_map(
        shards,
        mesh=mesh,
        in_specs=(
            P(AXES, None, None),
            P(),
            P(),
            P(),
            P(),
            P(),
            P(AXES, None),
            P(AXES),
        ),
        out_specs=P(AXES, None, None),
        check_vma=False,
    )
```

time: 533 us -> 179 us (0.34); the launches traced: 524 us -> 178 us
  other arithmetic: 209 us -> 0 us
  local copies, waits for them, and re-layouts: 132 us -> 7.45 us
  blocking collectives: 99.4 us -> 0 us
  waiting for transfers between devices: 43 us -> 95.3 us
  Pallas kernels: 0 us -> 34.8 us
  starting transfers between devices: 11 us -> 40.3 us
  matrix products: 28.9 us -> 0 us
    another operation x7 -> x0, other arithmetic: 173 us -> none  [the longest x4 94.6 us: analyse(): lowers = jnp.linalg.cholesky(stacked)]
    all_to_all x1 -> x0, blocking collectives: 99.4 us -> none  [shards(): lax.all_to_all(result, ('mem', 'patch'), split_axis=0, concat_axis=2, til...]
    unnamed x53 -> x44, local copies, waits for them, and re-layouts: 53.4 us -> 7.45 us
    pallas_call x0 -> x13, Pallas kernels: none -> 34.8 us  [the longest x10 24.8 us: call(): pl.pallas_call(kernel, grid=(1,), in_specs=[pl.BlockSpec(memory_space=plt...]
    gather x15 -> x0, local copies, waits for them, and re-layouts: 34.6 us -> none  [the longest x1 4.68 us: analyse(): offset = columns[lists].astype(f32) - centre[:, None]]
    ppermute x2 -> x6, waiting for transfers between devices: 0.01 us -> 32.8 us  [shards(): cross = lambda array: lax.ppermute(array, AXES, pairs)]
    dot_general x19 -> x0, matrix products: 27.9 us -> none  [the longest x1 10.2 us: analyse(): lax.dot_general(mix_full, masked, (((0,), (0,)), ((), ())), precision=hig...]
    all_to_all x3 -> x0, local copies, waits for them, and re-layouts: 25.3 us -> none  [the longest x1 20 us: shards(): lax.all_to_all(ensemble, ('mem', 'patch'), split_axis=2, concat_axis=0, t...]
  transfers between devices with their start and end apart: 3 -> 10, of which waited for: 1 -> 8; matrix products, arithmetic and copies ran while one was open for 11% -> 0% of each run, Pallas kernels for 0% -> 14%
where the time goes in v1:
time: 179 us; the launch traced here: 178 us
  waiting for transfers between devices  95.3 us (53%)
  starting transfers between devices  40.3 us (23%)
  Pallas kernels  34.8 us (19%)
  local copies, waits for them, and re-layouts  7.45 us (4%)
    all_to_all x1, waiting for transfers between devices, shards(): sum_x, x0 = sums(side, swap(send0), coarse_list, later)  36.3 us
    ppermute x6, waiting for transfers between devices, shards(): cross = lambda array: lax.ppermute(array, AXES, pairs)  32.8 us
    pallas_call x10, Pallas kernels, call(): pl.pallas_call(kernel, grid=(1,), in_specs=[pl.BlockSpec(memory_space=plt...  24.8 us
    all_to_all x1, waiting for transfers between devices, shards(): result = join(swap(result1), 1, 2, join(back0, 0, 2, None))  21.3 us
    ppermute x6, starting transfers between devices, shards(): cross = lambda array: lax.ppermute(array, AXES, pairs)  16 us
    unnamed x44, local copies, waits for them, and re-layouts  7.45 us
    all_to_all x1, starting transfers between devices, shards(): result = join(swap(result1), 1, 2, join(back0, 0, 2, None))  7 us
    pallas_call x1, Pallas kernels, split(): pl.pallas_call(functools.partial(split_kernel, per_step, width), grid=(de...  6.98 us
  transfers between devices with their start and end apart: 10, of which 8 were waited for; matrix products, arithmetic and copies ran while one was open for 0% of the time, Pallas kernels for 14%

profile of v1, /device:TPU:0, one launch (start us, length us, event | category | flops | bytes accessed | tf_op | source)
XLA Modules:
  0.0 178.2 jit_solution(17848406045676725214)
XLA Ops:
  0.0 7.0 %split.1 = (bf16[16,2,10,32,128]{4,3,2,1,0:T(8,128)(2,1)}, bf16[16,2,6,32,128]{4,3,2,1,0:T(8,128)(2,1)}) custom-call(bf16[12,32,4096]{2,1,0:T(8,128)(2,1)} %bitcast.11, s32[32,128]{1,0:T(8,128)} %bitcast.12, s32[32,128]{1,0:T(8,128)} %bitcast.7), custom_call_target="tpu_custom_call" | custom-call | tf_op jit(solution)/shard_map/split/pallas_call | solution.py:179
  7.0 0.0 copy-start.5
  7.0 6.3 %all-to-all-start = ((bf16[16,2,10,32,128]{4,3,2,1,0:T(8,128)(2,1)}), bf16[16,2,10,32,128]{4,3,2,1,0:T(8,128)(2,1)S(1)}, u32[]{:S(2)}, u32[]{:S(2)}) async-start(bf16[16,2,10,32,128]{4,3,2,1,0:T(8,128)(2,1)} %get-tuple-element.29), calls=%async_computation | async-start | bytes 5242880 | tf_op jit(solution)/shard_map/all_to_all | solution.py:547
  13.3 36.3 %all-to-all-done.x_ref = bf16[16,2,10,32,128]{4,3,2,1,0:T(8,128)(2,1)S(1)} async-done(((bf16[16,2,10,32,128]{4,3,2,1,0:T(8,128)(2,1)}), bf16[16,2,10,32,128]{4,3,2,1,0:T(8,128)(2,1)S(1)}, u32[]{:S(2)}, u32[]{:S(2)}) %all-to-all-start) | async-done | bytes 2621472 | tf_op jit(solution)/shard_map/all_to_all | solution.py:547
  49.6 0.0 copy-done.5
  49.6 0.6 sums.1
  50.2 0.0 copy-start.8
  50.2 2.7 %collective-permute-start = (f32[2,19,128]{2,1,0:T(8,128)S(1)}, f32[2,19,128]{2,1,0:T(8,128)S(1)}, u32[]{:S(2)}, u32[]{:S(2)}) collective-permute-start(f32[2,19,128]{2,1,0:T(8,128)S(1)} %get-tuple-element.31.sum_ref.rest_0_), channel_id=1, source_target_pairs={{0,16},{1,17},{2,18},{3,19},{4,20},{5,21},{6,22},{7,23},{8,24},{9,... | collective-permute-start | bytes 58376 | tf_op jit(solution)/shard_map/ppermute | solution.py:541
  52.9 2.4 %collective-permute-done.got_ref.rest_1_ = f32[2,19,128]{2,1,0:T(8,128)S(1)} collective-permute-done((f32[2,19,128]{2,1,0:T(8,128)S(1)}, f32[2,19,128]{2,1,0:T(8,128)S(1)}, u32[]{:S(2)}, u32[]{:S(2)}) %collective-permute-start) | collective-permute-done | bytes 19488 | tf_op jit(solution)/shard_map/ppermute | solution.py:541
  55.3 1.4 picks.2
  56.6 0.0 copy-start.10
  56.7 2.4 %collective-permute-start.1 = (f32[264,128]{1,0:T(8,128)S(1)}, f32[264,128]{1,0:T(8,128)S(1)}, u32[]{:S(2)}, u32[]{:S(2)}) collective-permute-start(f32[264,128]{1,0:T(8,128)S(1)} %get-tuple-element.32), channel_id=1, source_target_pairs={{0,16},{1,17},{2,18},{3,19},{4,20},{5,21},{6,22},{7,23},{8,24},{9,... | collective-permute-start | bytes 405512 | tf_op jit(solution)/shard_map/ppermute | solution.py:541
  59.1 1.4 picks.3
  60.4 0.0 copy-done.10
  60.5 0.0 copy-start.13
  60.5 0.0 copy-start.16
  60.5 0.0 copy-done.8
  60.5 1.0 project.2
  61.5 0.0 copy-done.13
  61.5 0.0 copy-done.16
  61.5 0.0 copy-start.2
  61.5 0.0 copy-start.3
  61.6 0.0 copy-start.4
  61.6 0.0 copy-start.6
  61.6 0.0 copy-start.7
  61.6 0.7 collective-permute-start.2
  62.3 7.0 %collective-permute-done.1.got_ref = f32[264,128]{1,0:T(8,128)S(1)} collective-permute-done((f32[264,128]{1,0:T(8,128)S(1)}, f32[264,128]{1,0:T(8,128)S(1)}, u32[]{:S(2)}, u32[]{:S(2)}) %collective-permute-start.1) | collective-permute-done | bytes 135200 | tf_op jit(solution)/shard_map/ppermute | solution.py:541
  69.2 6.8 %all-to-all-start.1 = ((bf16[16,2,6,32,128]{4,3,2,1,0:T(8,128)(2,1)}), bf16[16,2,6,32,128]{4,3,2,1,0:T(8,128)(2,1)S(1)}, u32[]{:S(2)}, u32[]{:S(2)}) async-start(bf16[16,2,6,32,128]{4,3,2,1,0:T(8,128)(2,1)} %get-tuple-element.44), calls=%async_computation.1 | async-start | bytes 3145728 | tf_op jit(solution)/shard_map/all_to_all | solution.py:556
  76.1 0.0 copy-done.2
  76.1 0.0 copy-done.3
  76.1 0.0 copy-done.4
  76.1 0.0 copy-done.6
  76.1 0.0 copy-done.7
  76.1 15.7 %weights.1 = (f32[512,128]{1,0:T(8,128)S(1)}, f32[128,128]{1,0:T(8,128)S(1)}) custom-call(s32[1]{0:T(128)} %bitcast.me_ref, s32[32]{0:T(128)S(1)} %copy-done.6, s32[4]{0:T(128)S(1)} %copy-done.7, s32[4,128]{1,0:T(4,128)S(1)} %copy-done.5, f32[32,128]{1,0:T(8,128)S(1)} %bitcast.9, f32[32,128]{1,0:T(8,128)S(1)} %bitcast.10, s32[32,128]{1,0:T(8,128)S(1)} %bitcast.8, ...), custom_call_target="tpu_custom_call" | custom-call | flops 80000000000 | bytes 1048576 | tf_op jit(solution)/shard_map/weights/pallas_call | solution.py:201
  91.8 0.0 collective-permute-done.2.got_ref
  91.8 0.9 spread.2.rest_2_
  92.7 0.0 copy-done.20
  92.7 3.3 %collective-permute-start.3 = (bf16[144,768]{1,0:T(8,128)(2,1)S(1)}, bf16[144,768]{1,0:T(8,128)(2,1)S(1)}, u32[]{:S(2)}, u32[]{:S(2)}) collective-permute-start(bf16[144,768]{1,0:T(8,128)(2,1)S(1)} %spread.2.rest_2_), channel_id=1, source_target_pairs={{0,16},{1,17},{2,18},{3,19},{4,20},{5,21},{6,22},{7,23},{8,24},{9,... | collective-permute-start | bytes 663560 | tf_op jit(solution)/shard_map/ppermute | solution.py:541
  96.0 2.9 %all-to-all-done.1.x_ref = bf16[16,2,6,32,128]{4,3,2,1,0:T(8,128)(2,1)S(1)} async-done(((bf16[16,2,6,32,128]{4,3,2,1,0:T(8,128)(2,1)}), bf16[16,2,6,32,128]{4,3,2,1,0:T(8,128)(2,1)S(1)}, u32[]{:S(2)}, u32[]{:S(2)}) %all-to-all-start.1) | async-done | bytes 1572896 | tf_op jit(solution)/shard_map/all_to_all | solution.py:556
  98.9 1.0 copy-done.17
  99.9 1.0 project.3
  100.9 0.0 copy-start.18
  100.9 3.8 %collective-permute-start.4 = (bf16[128,768]{1,0:T(8,128)(2,1)S(1)}, bf16[128,768]{1,0:T(8,128)(2,1)S(1)}, u32[]{:S(2)}, u32[]{:S(2)}) collective-permute-start(bf16[128,768]{1,0:T(8,128)(2,1)S(1)} %get-tuple-element.50), channel_id=1, source_target_pairs={{0,16},{1,17},{2,18},{3,19},{4,20},{5,21},{6,22},{7,23},{8,24},{9,... | collective-permute-start | bytes 589832 | tf_op jit(solution)/shard_map/ppermute | solution.py:541
  104.7 6.5 %collective-permute-done.3.rest_3_ = bf16[144,768]{1,0:T(8,128)(2,1)S(1)} collective-permute-done((bf16[144,768]{1,0:T(8,128)(2,1)S(1)}, bf16[144,768]{1,0:T(8,128)(2,1)S(1)}, u32[]{:S(2)}, u32[]{:S(2)}) %collective-permute-start.3) | collective-permute-done | bytes 221216 | tf_op jit(solution)/shard_map/ppermute | solution.py:541
  111.2 1.0 copy-done.11
  112.3 1.0 copy-done.14
  113.3 1.0 update.2
  114.4 0.0 copy-start
  114.4 1.1 copy-done
  115.5 0.0 collective-permute-done.4.got_ref
  115.5 4.1 %all-to-all-start.3 = ((bf16[16,2,6,32,128]{4,3,2,1,0:T(8,128)(2,1)}), bf16[16,2,6,32,128]{4,3,2,1,0:T(8,128)(2,1)S(1)}, u32[]{:S(2)}, u32[]{:S(2)}) async-start(bf16[16,2,6,32,128]{4,3,2,1,0:T(8,128)(2,1)} %copy-done), calls=%async_computation.3 | async-start | bytes 3145728 | tf_op jit(solution)/shard_map/all_to_all | solution.py:579
  119.6 0.0 copy-start.19
  119.6 1.0 copy-done.19
  120.6 0.9 copy-done.21
  121.6 0.9 spread.3.rest_2_
  122.5 3.3 %collective-permute-start.5 = (bf16[144,768]{1,0:T(8,128)(2,1)S(1)}, bf16[144,768]{1,0:T(8,128)(2,1)S(1)}, u32[]{:S(2)}, u32[]{:S(2)}) collective-permute-start(bf16[144,768]{1,0:T(8,128)(2,1)S(1)} %spread.3.rest_2_), channel_id=1, source_target_pairs={{0,16},{1,17},{2,18},{3,19},{4,20},{5,21},{6,22},{7,23},{8,24},{9,... | collective-permute-start | bytes 663560 | tf_op jit(solution)/shard_map/ppermute | solution.py:541
  125.7 16.9 %collective-permute-done.5.rest_3_ = bf16[144,768]{1,0:T(8,128)(2,1)S(1)} collective-permute-done((bf16[144,768]{1,0:T(8,128)(2,1)S(1)}, bf16[144,768]{1,0:T(8,128)(2,1)S(1)}, u32[]{:S(2)}, u32[]{:S(2)}) %collective-permute-start.5) | collective-permute-done | bytes 221216 | tf_op jit(solution)/shard_map/ppermute | solution.py:541
  142.6 1.0 update.3
  143.7 1.2 copy-done.1
  144.8 2.1 %all-to-all-done.3.in_ref = bf16[16,2,6,32,128]{4,3,2,1,0:T(8,128)(2,1)S(1)} async-done(((bf16[16,2,6,32,128]{4,3,2,1,0:T(8,128)(2,1)}), bf16[16,2,6,32,128]{4,3,2,1,0:T(8,128)(2,1)S(1)}, u32[]{:S(2)}, u32[]{:S(2)}) %all-to-all-start.3) | async-done | bytes 1572896 | tf_op jit(solution)/shard_map/all_to_all | solution.py:579
  146.9 7.0 %all-to-all-start.2 = ((bf16[16,2,6,32,128]{4,3,2,1,0:T(8,128)(2,1)}), bf16[16,2,6,32,128]{4,3,2,1,0:T(8,128)(2,1)S(1)}, u32[]{:S(2)}, u32[]{:S(2)}) async-start(bf16[16,2,6,32,128]{4,3,2,1,0:T(8,128)(2,1)} %copy-done.1), calls=%async_computation.2 | async-start | bytes 3145728 | tf_op jit(solution)/shard_map/all_to_all | solution.py:581
  153.9 1.5 join.2.rest_0_
  155.4 21.3 %all-to-all-done.2.in_ref = bf16[16,2,6,32,128]{4,3,2,1,0:T(8,128)(2,1)S(1)} async-done(((bf16[16,2,6,32,128]{4,3,2,1,0:T(8,128)(2,1)}), bf16[16,2,6,32,128]{4,3,2,1,0:T(8,128)(2,1)S(1)}, u32[]{:S(2)}, u32[]{:S(2)}) %all-to-all-start.2) | async-done | bytes 1572896 | tf_op jit(solution)/shard_map/all_to_all | solution.py:581
  176.7 1.5 join.3
  (13 shorter events, 0.0 us)
Async XLA Ops:
  7.0 42.6 %copy-start.5 = (s32[4,128]{1,0:T(4,128)S(1)}, s32[4,128]{1,0:T(4,128)}, u32[]{:S(2)}) copy-start(s32[4,128]{1,0:T(4,128)} %lists_ref.7) | copy-start | bytes 6148
  7.0 42.6 %all-to-all-start = ((bf16[16,2,10,32,128]{4,3,2,1,0:T(8,128)(2,1)}), bf16[16,2,10,32,128]{4,3,2,1,0:T(8,128)(2,1)S(1)}, u32[]{:S(2)}, u32[]{:S(2)}) async-start(bf16[16,2,10,32,128]{4,3,2,1,0:T(8,128)(2,1)} %get-tuple-element.29), calls=%async_computation | async-start | bytes 5242880 | tf_op jit(solution)/shard_map/all_to_all | solution.py:547
  50.2 10.3 %copy-start.8 = (bf16[16,2,10,32,128]{4,3,2,1,0:T(8,128)(2,1)}, bf16[16,2,10,32,128]{4,3,2,1,0:T(8,128)(2,1)S(1)}, u32[]{:S(2)}) copy-start(bf16[16,2,10,32,128]{4,3,2,1,0:T(8,128)(2,1)S(1)} %get-tuple-element.30.rows_ref.x_ref) | copy-start | bytes 7864324
  50.2 5.1 %collective-permute-start = (f32[2,19,128]{2,1,0:T(8,128)S(1)}, f32[2,19,128]{2,1,0:T(8,128)S(1)}, u32[]{:S(2)}, u32[]{:S(2)}) collective-permute-start(f32[2,19,128]{2,1,0:T(8,128)S(1)} %get-tuple-element.31.sum_ref.rest_0_), channel_id=1, source_target_pairs={{0,16},{1,17},{2,18},{3,19},{4,20},{5,21},{6,22},{7,23},{8,24},{9,... | collective-permute-start | bytes 58376 | tf_op jit(solution)/shard_map/ppermute | solution.py:541
  56.6 3.8 %copy-start.10 = (bf16[512,512]{1,0:T(8,128)(2,1)}, bf16[512,512]{1,0:T(8,128)(2,1)S(1)}, u32[]{:S(2)}) copy-start(bf16[512,512]{1,0:T(8,128)(2,1)S(1)} %get-tuple-element.47.rest_1_) | copy-start | bytes 1572868
  56.7 12.6 %collective-permute-start.1 = (f32[264,128]{1,0:T(8,128)S(1)}, f32[264,128]{1,0:T(8,128)S(1)}, u32[]{:S(2)}, u32[]{:S(2)}) collective-permute-start(f32[264,128]{1,0:T(8,128)S(1)} %get-tuple-element.32), channel_id=1, source_target_pairs={{0,16},{1,17},{2,18},{3,19},{4,20},{5,21},{6,22},{7,23},{8,24},{9,... | collective-permute-start | bytes 405512 | tf_op jit(solution)/shard_map/ppermute | solution.py:541
  60.5 1.1 copy-start.13
  60.5 1.1 copy-start.16
  61.5 14.6 %copy-start.2 = (s32[4096]{0:T(1024)S(1)}, s32[4096]{0:T(1024)}, u32[]{:S(2)}) copy-start(s32[4096]{0:T(1024)} %param.9) | copy-start | bytes 49156
  61.5 14.6 %copy-start.3 = (f32[4096]{0:T(1024)S(1)}, f32[4096]{0:T(1024)}, u32[]{:S(2)}) copy-start(f32[4096]{0:T(1024)} %param.11) | copy-start | bytes 49156
  61.6 14.6 %copy-start.4 = (f32[4096]{0:T(1024)S(1)}, f32[4096]{0:T(1024)}, u32[]{:S(2)}) copy-start(f32[4096]{0:T(1024)} %param.12) | copy-start | bytes 49156
  61.6 14.6 %copy-start.6 = (s32[32]{0:T(128)S(1)}, s32[32]{0:T(128)}, u32[]{:S(2)}) copy-start(s32[32]{0:T(128)} %obs_count_ref.1) | copy-start | bytes 388
  61.6 14.6 %copy-start.7 = (s32[4]{0:T(128)S(1)}, s32[4]{0:T(128)}, u32[]{:S(2)}) copy-start(s32[4]{0:T(128)} %live_ref.1) | copy-start | bytes 52
  61.6 30.2 %collective-permute-start.2 = (bf16[128,768]{1,0:T(8,128)(2,1)S(1)}, bf16[128,768]{1,0:T(8,128)(2,1)S(1)}, u32[]{:S(2)}, u32[]{:S(2)}) collective-permute-start(bf16[128,768]{1,0:T(8,128)(2,1)S(1)} %get-tuple-element.38), channel_id=1, source_target_pairs={{0,16},{1,17},{2,18},{3,19},{4,20},{5,21},{6,22},{7,23},{8,24},{9,... | collective-permute-start | bytes 589832 | tf_op jit(solution)/shard_map/ppermute | solution.py:541
  69.2 29.6 %all-to-all-start.1 = ((bf16[16,2,6,32,128]{4,3,2,1,0:T(8,128)(2,1)}), bf16[16,2,6,32,128]{4,3,2,1,0:T(8,128)(2,1)S(1)}, u32[]{:S(2)}, u32[]{:S(2)}) async-start(bf16[16,2,6,32,128]{4,3,2,1,0:T(8,128)(2,1)} %get-tuple-element.44), calls=%async_computation.1 | async-start | bytes 3145728 | tf_op jit(solution)/shard_map/all_to_all | solution.py:556
  91.8 0.9 copy-start.20
  92.7 18.5 %collective-permute-start.3 = (bf16[144,768]{1,0:T(8,128)(2,1)S(1)}, bf16[144,768]{1,0:T(8,128)(2,1)S(1)}, u32[]{:S(2)}, u32[]{:S(2)}) collective-permute-start(bf16[144,768]{1,0:T(8,128)(2,1)S(1)} %spread.2.rest_2_), channel_id=1, source_target_pairs={{0,16},{1,17},{2,18},{3,19},{4,20},{5,21},{6,22},{7,23},{8,24},{9,... | collective-permute-start | bytes 663560 | tf_op jit(solution)/shard_map/ppermute | solution.py:541
  98.9 1.0 copy-start.17
  99.9 11.3 %copy-start.9 = (bf16[16,2,10,32,128]{4,3,2,1,0:T(8,128)(2,1)S(1)}, bf16[16,2,10,32,128]{4,3,2,1,0:T(8,128)(2,1)}, u32[]{:S(2)}) copy-start(bf16[16,2,10,32,128]{4,3,2,1,0:T(8,128)(2,1)} %copy-done.8) | copy-start | bytes 7864324
  100.9 13.4 %copy-start.18 = (f32[128,768]{1,0:T(8,128)}, f32[128,768]{1,0:T(8,128)S(1)}, u32[]{:S(2)}) copy-start(f32[128,768]{1,0:T(8,128)S(1)} %get-tuple-element.48.mine_ref) | copy-start | bytes 1179652
  100.9 14.6 %collective-permute-start.4 = (bf16[128,768]{1,0:T(8,128)(2,1)S(1)}, bf16[128,768]{1,0:T(8,128)(2,1)S(1)}, u32[]{:S(2)}, u32[]{:S(2)}) collective-permute-start(bf16[128,768]{1,0:T(8,128)(2,1)S(1)} %get-tuple-element.50), channel_id=1, source_target_pairs={{0,16},{1,17},{2,18},{3,19},{4,20},{5,21},{6,22},{7,23},{8,24},{9,... | collective-permute-start | bytes 589832 | tf_op jit(solution)/shard_map/ppermute | solution.py:541
  111.2 1.0 copy-start.11
  112.3 1.0 copy-start.14
  114.4 1.1 copy-start
  115.5 31.4 %all-to-all-start.3 = ((bf16[16,2,6,32,128]{4,3,2,1,0:T(8,128)(2,1)}), bf16[16,2,6,32,128]{4,3,2,1,0:T(8,128)(2,1)S(1)}, u32[]{:S(2)}, u32[]{:S(2)}) async-start(bf16[16,2,6,32,128]{4,3,2,1,0:T(8,128)(2,1)} %copy-done), calls=%async_computation.3 | async-start | bytes 3145728 | tf_op jit(solution)/shard_map/all_to_all | solution.py:579
  119.6 1.0 copy-start.19
  120.6 0.9 copy-start.21
  121.6 21.1 %copy-start.12 = (bf16[512,512]{1,0:T(8,128)(2,1)S(1)}, bf16[512,512]{1,0:T(8,128)(2,1)}, u32[]{:S(2)}) copy-start(bf16[512,512]{1,0:T(8,128)(2,1)} %copy-done.10) | copy-start | bytes 1572868
  121.6 21.1 %copy-start.15 = (bf16[512,512]{1,0:T(8,128)(2,1)S(1)}, bf16[512,512]{1,0:T(8,128)(2,1)}, u32[]{:S(2)}) copy-start(bf16[512,512]{1,0:T(8,128)(2,1)} %copy-done.13) | copy-start | bytes 1572868
  122.5 20.2 %collective-permute-start.5 = (bf16[144,768]{1,0:T(8,128)(2,1)S(1)}, bf16[144,768]{1,0:T(8,128)(2,1)S(1)}, u32[]{:S(2)}, u32[]{:S(2)}) collective-permute-start(bf16[144,768]{1,0:T(8,128)(2,1)S(1)} %spread.3.rest_2_), channel_id=1, source_target_pairs={{0,16},{1,17},{2,18},{3,19},{4,20},{5,21},{6,22},{7,23},{8,24},{9,... | collective-permute-start | bytes 663560 | tf_op jit(solution)/shard_map/ppermute | solution.py:541
  143.7 1.2 copy-start.1
  146.9 29.8 %all-to-all-start.2 = ((bf16[16,2,6,32,128]{4,3,2,1,0:T(8,128)(2,1)}), bf16[16,2,6,32,128]{4,3,2,1,0:T(8,128)(2,1)S(1)}, u32[]{:S(2)}, u32[]{:S(2)}) async-start(bf16[16,2,6,32,128]{4,3,2,1,0:T(8,128)(2,1)} %copy-done.1), calls=%async_computation.2 | async-start | bytes 3145728 | tf_op jit(solution)/shard_map/all_to_all | solution.py:581
